TPU v7x, 512 devices: a whole 4x8x8 slice. The times are simulated.
512 devices in a mesh: dp: 64 (over z_lo, x, y), tensor: 8 (over z_hi, core).
Axes of the slice: x: 4, y: 8, z: 8 (z_hi: 4, z_lo: 2; z = z_hi * 2 + z_lo), core: 2. Of those that a mesh axis runs over, the one named last changes fastest.
Arguments:
- image_embedding_matrix: float32 [1152, 32768], P('tensor', 'dp'), may hold values from -0.1875 to 0.1875
- words_embedding_matrix: float32 [1152, 32768], P('tensor', 'dp'), may hold values from -0.1875 to 0.1875
- natural_exponent_heat: float32 [1], replicated, may hold values from 2 to 2.5
- offset_term_array: float32 [1], replicated, may hold values from -2 to -1
Outputs:
- image_grad: float32 [1152, 32768], P('tensor', 'dp')
- text_grad: float32 [1152, 32768], P('tensor', 'dp')
All inputs are finite; a program needn't handle non-finite values.
Results may differ from a plain program's by a relative error of at most 0.0001.
Values sent between devices are 32-bit elements; how exact they have to be, the bound alone decides.
A program may use at most 64 MiB of HBM per device.

v0:
```python
import jax
import jax.numpy as jnp
from jax import lax
from jax.sharding import PartitionSpec as P

SHIFTS = 4


def from_behind(block, axis, distance):
    devices = range(lax.axis_size(axis))
    route = [((i - distance) % len(devices), i) for i in devices]
    return lax.ppermute(block, axis, route)


def tile_loss_entries(
    image_embedding_matrix,
    words_segment,
    heat_factor,
    segment_offset_amount,
    matched_target_indicator,
):
    partial_value = lax.dot_general(
        image_embedding_matrix,
        words_segment,
        (((0,), (0,)), ((), ())),
        precision=lax.Precision.HIGHEST,
        preferred_element_type=jnp.float32,
    )
    segment_objective_total = lax.psum(partial_value, "tensor")
    squashing_slope_factor = jax.nn.sigmoid(
        heat_factor * segment_objective_total + segment_offset_amount
    )
    if matched_target_indicator:
        row_ids = lax.broadcasted_iota(jnp.int32, squashing_slope_factor.shape, 0)
        col_ids = lax.broadcasted_iota(jnp.int32, squashing_slope_factor.shape, 1)
        squashing_slope_factor = squashing_slope_factor - jnp.where(
            row_ids == col_ids, 1.0, 0.0
        ).astype(jnp.float32)
    image_partial_share = heat_factor * lax.dot_general(
        words_segment,
        squashing_slope_factor,
        (((1,), (1,)), ((), ())),
        precision=lax.Precision.HIGHEST,
        preferred_element_type=jnp.float32,
    )
    words_partial_share = heat_factor * jnp.dot(
        image_embedding_matrix,
        squashing_slope_factor,
        precision=lax.Precision.HIGHEST,
        preferred_element_type=jnp.float32,
    )
    return (image_partial_share, words_partial_share)


def shards(
    image_embedding_matrix, words_embedding_matrix, natural_exponent_heat, offset_term_array
):
    heat_factor = jnp.exp(natural_exponent_heat[0])
    segment_offset_amount = offset_term_array[0]
    image_slope_total = jnp.zeros(image_embedding_matrix.shape, jnp.float32)
    travelling = jnp.zeros(words_embedding_matrix.shape, jnp.float32)
    words_segment = words_embedding_matrix
    for shift_counter in range(SHIFTS):
        if shift_counter > 0:
            words_segment = from_behind(words_segment, "dp", 1)
        image_partial_share, words_partial_share = tile_loss_entries(
            image_embedding_matrix,
            words_segment,
            heat_factor,
            segment_offset_amount,
            shift_counter == 0,
        )
        image_slope_total = image_slope_total + image_partial_share
        if shift_counter > 0:
            travelling = from_behind(travelling, "dp", 1)
        travelling = travelling + words_partial_share
    text_total = from_behind(travelling, "dp", -(SHIFTS - 1))
    return (image_slope_total, text_total)


def solution(mesh):
    return jax.shard_map(
        shards,
        mesh=mesh,
        in_specs=(P("tensor", "dp"), P("tensor", "dp"), P(), P()),
        out_specs=(P("tensor", "dp"), P("tensor", "dp")),
        check_vma=False,
    )
```

profile of v0, /device:TPU:128, one launch (start us, length us, event | category | flops | bytes accessed | tf_op | source)
XLA Modules:
  0.0 251.9 jit_solution(7954430026358777063)
XLA Ops:
  7.2 3.6 %collective-permute-start = (f32[144,512]{1,0:T(8,128)}, f32[144,512]{1,0:T(8,128)S(1)}, u32[]{:S(2)}, u32[]{:S(2)}) collective-permute-start(f32[144,512]{1,0:T(8,128)} %param.5), channel_id=1, source_target_pairs={{504,0},{0,8},{8,16},{16,24},{24,32},{32,40},{40,48},{48,56},{56,6... | collective-permute-start | bytes 884744 | tf_op jit(solution)/shard_map/ppermute | solution.py:12
  10.8 13.1 %collective-permute-done = f32[144,512]{1,0:T(8,128)S(1)} collective-permute-done((f32[144,512]{1,0:T(8,128)}, f32[144,512]{1,0:T(8,128)S(1)}, u32[]{:S(2)}, u32[]{:S(2)}) %collective-permute-start) | collective-permute-done | bytes 294944 | tf_op jit(solution)/shard_map/ppermute | solution.py:12
  23.9 1.9 collective-permute-start.1
  25.9 3.0 %fusion.14 = f32[512,512]{1,0:T(8,128)} fusion(f32[144,512]{1,0:T(8,128)S(1)} %copy-done, f32[144,512]{1,0:T(8,128)} %param.5), kind=kOutput, calls=%fused_computation.26 | convolution fusion | flops 452984832 | bytes 1638400 | tf_op jit(solution)/shard_map/dot_general | solution.py:22
  28.9 9.3 %collective-permute-done.1 = f32[144,512]{1,0:T(8,128)S(1)} collective-permute-done((f32[144,512]{1,0:T(8,128)S(1)}, f32[144,512]{1,0:T(8,128)S(1)}, u32[]{:S(2)}, u32[]{:S(2)}) %collective-permute-start.1) | collective-permute-done | bytes 294944 | tf_op jit(solution)/shard_map/ppermute | solution.py:12
  38.2 1.9 collective-permute-start.2
  40.2 2.1 fusion.15
  42.3 2.1 fusion.16
  44.4 7.2 %collective-permute-done.2 = f32[144,512]{1,0:T(8,128)S(1)} collective-permute-done((f32[144,512]{1,0:T(8,128)S(1)}, f32[144,512]{1,0:T(8,128)S(1)}, u32[]{:S(2)}, u32[]{:S(2)}) %collective-permute-start.2) | collective-permute-done | bytes 294944 | tf_op jit(solution)/shard_map/ppermute | solution.py:12
  51.6 2.1 fusion.17
  55.1 116.6 %all-reduce.3.cloned.1.call-done = (f32[512,512]{1,0:T(8,128)}, f32[512,512]{1,0:T(8,128)}, f32[512,512]{1,0:T(8,128)}, f32[512,512]{1,0:T(8,128)}) async-done(((f32[512,512]{1,0:T(8,128)}, f32[512,512]{1,0:T(8,128)}, f32[512,512]{1,0:T(8,128)}, f32[512,512]{1,0:T(8,128)}), (f32[512,512]{1,0:T(8,128)}, f32[512,512]{1,0:T(8,128)}, f32[512,512]{1,0:T(8,128)}, ...) | async-done | bytes 4194320 | tf_op jit(solution)/shard_map/psum | solution.py:29
  171.7 2.3 fusion.2
  174.0 4.2 %collective-permute-start.3 = (f32[144,512]{1,0:T(8,128)S(1)}, f32[144,512]{1,0:T(8,128)S(1)}, u32[]{:S(2)}, u32[]{:S(2)}) collective-permute-start(f32[144,512]{1,0:T(8,128)S(1)} %fusion.2), channel_id=1, source_target_pairs={{504,0},{0,8},{8,16},{16,24},{24,32},{32,40},{40,48},{48,56},{56,6... | collective-permute-start | bytes 884744 | tf_op jit(solution)/shard_map/ppermute | solution.py:12
  179.2 9.6 %collective-permute-done.3 = f32[144,512]{1,0:T(8,128)S(1)} collective-permute-done((f32[144,512]{1,0:T(8,128)S(1)}, f32[144,512]{1,0:T(8,128)S(1)}, u32[]{:S(2)}, u32[]{:S(2)}) %collective-permute-start.3) | collective-permute-done | bytes 294944 | tf_op jit(solution)/shard_map/ppermute | solution.py:12
  189.8 1.9 collective-permute-start.4
  191.8 1.5 fusion.13
  193.3 12.5 %collective-permute-done.4 = f32[144,512]{1,0:T(8,128)S(1)} collective-permute-done((f32[144,512]{1,0:T(8,128)S(1)}, f32[144,512]{1,0:T(8,128)S(1)}, u32[]{:S(2)}, u32[]{:S(2)}) %collective-permute-start.4) | collective-permute-done | bytes 294944 | tf_op jit(solution)/shard_map/ppermute | solution.py:12
  205.9 1.9 collective-permute-start.5
  208.8 1.4 convolution_add_fusion.2
  210.2 10.8 %collective-permute-done.5 = f32[144,512]{1,0:T(8,128)S(1)} collective-permute-done((f32[144,512]{1,0:T(8,128)S(1)}, f32[144,512]{1,0:T(8,128)S(1)}, u32[]{:S(2)}, u32[]{:S(2)}) %collective-permute-start.5) | collective-permute-done | bytes 294944 | tf_op jit(solution)/shard_map/ppermute | solution.py:12
  221.0 1.9 collective-permute-start.6
  223.0 1.4 convolution_add_fusion.1
  224.4 2.2 fusion.1
  226.6 17.7 %collective-permute-done.6 = f32[144,512]{1,0:T(8,128)S(1)} collective-permute-done((f32[144,512]{1,0:T(8,128)S(1)}, f32[144,512]{1,0:T(8,128)S(1)}, u32[]{:S(2)}, u32[]{:S(2)}) %collective-permute-start.6) | collective-permute-done | bytes 294944 | tf_op jit(solution)/shard_map/ppermute | solution.py:12
  (20 shorter events, 3.8 us)
Async XLA Ops:
  7.2 18.7 %copy-start = (f32[144,512]{1,0:T(8,128)S(1)}, f32[144,512]{1,0:T(8,128)}, u32[]{:S(2)}) copy-start(f32[144,512]{1,0:T(8,128)} %param.4) | copy-start | bytes 884740
  7.2 164.5 %all-reduce.3.cloned.1.call-start = ((), (), s32[]{:S(2)}) async-start(), calls=%async_computation | async-start | bytes 8388608 | tf_op jit(solution)/shard_map/psum | solution.py:29
  7.2 16.7 %collective-permute-start = (f32[144,512]{1,0:T(8,128)}, f32[144,512]{1,0:T(8,128)S(1)}, u32[]{:S(2)}, u32[]{:S(2)}) collective-permute-start(f32[144,512]{1,0:T(8,128)} %param.5), channel_id=1, source_target_pairs={{504,0},{0,8},{8,16},{16,24},{24,32},{32,40},{40,48},{48,56},{56,6... | collective-permute-start | bytes 884744 | tf_op jit(solution)/shard_map/ppermute | solution.py:12
  23.9 14.3 %collective-permute-start.1 = (f32[144,512]{1,0:T(8,128)S(1)}, f32[144,512]{1,0:T(8,128)S(1)}, u32[]{:S(2)}, u32[]{:S(2)}) collective-permute-start(f32[144,512]{1,0:T(8,128)S(1)} %collective-permute-done), channel_id=1, source_target_pairs={{504,0},{0,8},{8,16},{16,24},{24,32},{32,40},{40,48},{48,56},{56,6... | collective-permute-start | bytes 884744 | tf_op jit(solution)/shard_map/ppermute | solution.py:12
  38.2 13.4 %collective-permute-start.2 = (f32[144,512]{1,0:T(8,128)S(1)}, f32[144,512]{1,0:T(8,128)S(1)}, u32[]{:S(2)}, u32[]{:S(2)}) collective-permute-start(f32[144,512]{1,0:T(8,128)S(1)} %collective-permute-done.1), channel_id=1, source_target_pairs={{504,0},{0,8},{8,16},{16,24},{24,32},{32,40},{40,48},{48,56},{56,6... | collective-permute-start | bytes 884744 | tf_op jit(solution)/shard_map/ppermute | solution.py:12
  171.7 6.5 %copy-start.3 = (f32[512,512]{1,0:T(8,128)S(1)}, f32[512,512]{1,0:T(8,128)}, u32[]{:S(2)}) copy-start(f32[512,512]{1,0:T(8,128)} %get-tuple-element.4) | copy-start | bytes 3145732
  174.0 14.8 %collective-permute-start.3 = (f32[144,512]{1,0:T(8,128)S(1)}, f32[144,512]{1,0:T(8,128)S(1)}, u32[]{:S(2)}, u32[]{:S(2)}) collective-permute-start(f32[144,512]{1,0:T(8,128)S(1)} %fusion.2), channel_id=1, source_target_pairs={{504,0},{0,8},{8,16},{16,24},{24,32},{32,40},{40,48},{48,56},{56,6... | collective-permute-start | bytes 884744 | tf_op jit(solution)/shard_map/ppermute | solution.py:12
  178.2 10.6 %copy-start.4 = (f32[512,512]{1,0:T(8,128)S(1)}, f32[512,512]{1,0:T(8,128)}, u32[]{:S(2)}) copy-start(f32[512,512]{1,0:T(8,128)} %get-tuple-element.3) | copy-start | bytes 3145732
  188.8 2.9 %copy-start.1 = (f32[144,512]{1,0:T(8,128)S(1)}, f32[144,512]{1,0:T(8,128)}, u32[]{:S(2)}) copy-start(f32[144,512]{1,0:T(8,128)} %param.5) | copy-start | bytes 884740
  188.8 2.9 %copy-start.5 = (f32[512,512]{1,0:T(8,128)S(1)}, f32[512,512]{1,0:T(8,128)}, u32[]{:S(2)}) copy-start(f32[512,512]{1,0:T(8,128)} %get-tuple-element.2) | copy-start | bytes 3145732
  189.8 16.0 %collective-permute-start.4 = (f32[144,512]{1,0:T(8,128)S(1)}, f32[144,512]{1,0:T(8,128)S(1)}, u32[]{:S(2)}, u32[]{:S(2)}) collective-permute-start(f32[144,512]{1,0:T(8,128)S(1)} %fusion.4), channel_id=1, source_target_pairs={{504,0},{0,8},{8,16},{16,24},{24,32},{32,40},{40,48},{48,56},{56,6... | collective-permute-start | bytes 884744 | tf_op jit(solution)/shard_map/ppermute | solution.py:12
  191.8 16.0 %copy-start.2 = (f32[512,512]{1,0:T(8,128)S(1)}, f32[512,512]{1,0:T(8,128)}, u32[]{:S(2)}) copy-start(f32[512,512]{1,0:T(8,128)} %get-tuple-element.5) | copy-start | bytes 3145732
  205.9 15.1 %collective-permute-start.5 = (f32[144,512]{1,0:T(8,128)S(1)}, f32[144,512]{1,0:T(8,128)S(1)}, u32[]{:S(2)}, u32[]{:S(2)}) collective-permute-start(f32[144,512]{1,0:T(8,128)S(1)} %add.75), channel_id=1, source_target_pairs={{504,0},{0,8},{8,16},{16,24},{24,32},{32,40},{40,48},{48,56},{56,6... | collective-permute-start | bytes 884744 | tf_op jit(solution)/shard_map/ppermute | solution.py:12
  221.0 23.3 %collective-permute-start.6 = (f32[144,512]{1,0:T(8,128)S(1)}, f32[144,512]{1,0:T(8,128)S(1)}, u32[]{:S(2)}, u32[]{:S(2)}) collective-permute-start(f32[144,512]{1,0:T(8,128)S(1)} %add.76), channel_id=1, source_target_pairs={{24,0},{32,8},{40,16},{48,24},{56,32},{64,40},{72,48},{80,56},{88,... | collective-permute-start | bytes 884744 | tf_op jit(solution)/shard_map/ppermute | solution.py:12
Sparse Core Ops, SparseCore 0:
  53.9 117.7 all-reduce.2
where the time goes:
time: 252 us
  waiting for transfers between devices  197 us (78%)
  matrix products  21.1 us (8%)
  starting transfers between devices  17.4 us (7%)
  between operations  15.5 us (6%)
    psum x1, waiting for transfers between devices, tile_loss_entries(): segment_objective_total = lax.psum(partial_value, 'tensor')  117 us
    ppermute x7, waiting for transfers between devices, from_behind(): return lax.ppermute(block, axis, route)  80.4 us
    ppermute x7, starting transfers between devices, from_behind(): return lax.ppermute(block, axis, route)  17.4 us
    dot_general x4, matrix products, tile_loss_entries(): lax.dot_general(image_embedding_matrix, words_segment, (((0,), (0,)), (()...  9.36 us
    dot_general x4, matrix products, tile_loss_entries(): lax.dot_general(words_segment, squashing_slope_factor, (((1,), (1,)), (()...  6.5 us
    dot_general x4, matrix products, tile_loss_entries(): jnp.dot(image_embedding_matrix, squashing_slope_factor, precision=lax.Pre...  5.27 us
  transfers between devices with their start and end apart: 8, of which 8 were waited for; matrix products, arithmetic and copies ran while one was open for 6% of the time, Pallas kernels for 0%

commit v1 on v0

v1 whole, which is shorter than its diff:
```python
import jax
import jax.numpy as jnp
from jax import lax
from jax.experimental import pallas as pl
from jax.experimental.pallas import tpu as pltpu
from jax.sharding import PartitionSpec as P

SHIFTS = 4
N_Q = 4
MESH = pl.DeviceIdType.MESH
F32 = jnp.float32
BF16 = jnp.bfloat16

A_DIRECT_P, A_DIRECT_M, A_HALF_P, A_HALF_M, A_ON_P, A_ON_M = range(6)
T_SIB, T_OWN_P, T_OWN_M, T_SIB_P, T_SIB_M, T_ON_P, T_ON_M = range(6, 13)
B_FAR_P, B_FAR_M, B_NEAR_P, B_NEAR_M, B_SUM_P, B_SUM_M, B_SIB = range(13, 20)
E_DIRECT_P, E_DIRECT_M, E_HALF_P, E_HALF_M, E_ON_P, E_ON_M = range(20, 26)
G_SIB = 26
I_SIB = 30
CHAIN = 46
BACK = 58
N_SEMS = 70


def split(value):
    high = value.astype(BF16)
    return high, (value - high.astype(F32)).astype(BF16)


def dot3(a_high, a_low, b_high, b_low, dims):
    def one(a, b):
        return lax.dot_general(a, b, (dims, ((), ())), preferred_element_type=F32)

    return one(a_high, b_high) + (one(a_high, b_low) + one(a_low, b_high))


def kernel(
    n_dp,
    heat_ref,
    bias_ref,
    img_ref,
    txt_ref,
    gi_ref,
    gt_ref,
    text,
    image,
    t_high,
    t_low,
    i_high,
    i_low,
    g_text,
    g_image,
    g_other,
    back,
    far_in,
    near_in,
    keep,
    half_in,
    send_sem,
    recv_sem,
):
    d, rows = img_ref.shape
    half, piece = rows // 2, rows // N_Q
    dp, t = lax.axis_index("dp"), lax.axis_index("tensor")
    q, c = t // 2, t % 2
    o = 1 - c
    at = [lax.rem(q + r, N_Q) for r in range(N_Q)]
    sib = (dp, 2 * q + o)
    up, down = (dp, 2 * at[1] + c), (dp, 2 * at[3] + c)
    after, before = (lax.rem(dp + 1, n_dp), t), (lax.rem(dp + n_dp - 1, n_dp), t)
    started = []

    def send(index, src, dst, device):
        copy = pltpu.make_async_remote_copy(
            src_ref=src,
            dst_ref=dst,
            send_sem=send_sem.at[index],
            recv_sem=recv_sem.at[index],
            device_id=device,
            device_id_type=MESH,
        )
        copy.start()
        started.append(copy)

    def arrive(index, dst):
        pltpu.make_async_remote_copy(
            src_ref=dst,
            dst_ref=dst,
            send_sem=send_sem.at[index],
            recv_sem=recv_sem.at[index],
            device_id=sib,
            device_id_type=MESH,
        ).wait_recv()

    def piece_of(ref, r, first=0, count=None):
        cols = pl.ds(pl.multiple_of(at[r] * piece, piece), piece)
        return ref.at[pl.ds(first, d if count is None else count), cols]

    def half_of(ref, which):
        return ref.at[:, pl.ds(pl.multiple_of(which * half, half), half)]

    barrier = pltpu.get_barrier_semaphore()
    partners = (sib, up, down, after, before)
    for partner in partners:
        pl.semaphore_signal(barrier, inc=1, device_id=partner, device_id_type=MESH)
    pl.semaphore_wait(barrier, len(partners))

    h = d // 2
    send(A_HALF_P, piece_of(img_ref, 2, 0, h), half_in.at[0], up)
    send(A_HALF_M, piece_of(img_ref, 2, h, h), half_in.at[1], down)
    image[0, c, q] = piece_of(img_ref, 0)[...]

    def chain(k, r):
        if k < SHIFTS - 1:
            send(CHAIN + 4 * k + r, image.at[k, c, at[r]], image.at[k + 1, c, at[r]], before)
        send(I_SIB + 4 * k + r, image.at[k, c, at[r]], image.at[k, c, at[r]], sib)

    def chained(k, r):
        arrive(CHAIN + 4 * (k - 1) + r, image.at[k, c, at[r]])
        chain(k, r)

    chain(0, 0)
    send(A_DIRECT_P, piece_of(img_ref, 1), image.at[0, c, q], up)
    send(A_DIRECT_M, piece_of(img_ref, 3), image.at[0, c, q], down)
    send(T_SIB, half_of(txt_ref, o), text.at[c, q], sib)
    text[c, q] = half_of(txt_ref, c)[...]

    arrive(A_HALF_P, half_in.at[0])
    send(A_ON_P, half_in.at[0], image.at[0, c, at[3], pl.ds(0, h)], up)
    arrive(A_HALF_M, half_in.at[1])
    send(A_ON_M, half_in.at[1], image.at[0, c, at[1], pl.ds(h, h)], down)
    send(T_OWN_P, text.at[c, q], text.at[c, q], up)
    send(T_OWN_M, text.at[c, q], text.at[c, q], down)

    chained(1, 0)
    arrive(A_DIRECT_P, image.at[0, c, at[3]])
    chain(0, 3)
    arrive(A_DIRECT_M, image.at[0, c, at[1]])
    chain(0, 1)
    arrive(T_SIB, text.at[o, q])
    send(T_SIB_P, text.at[o, q], text.at[o, q], up)
    send(T_SIB_M, text.at[o, q], text.at[o, q], down)
    arrive(A_ON_P, image.at[0, c, at[2], pl.ds(0, h)])
    arrive(A_ON_M, image.at[0, c, at[2], pl.ds(h, h)])
    chain(0, 2)
    chained(2, 0)
    chained(1, 3)
    chained(1, 1)
    arrive(T_OWN_P, text.at[c, at[3]])
    send(T_ON_P, text.at[c, at[3]], text.at[c, at[3]], up)
    chained(1, 2)
    chained(3, 0)
    chained(2, 3)
    chained(2, 1)
    arrive(T_OWN_M, text.at[c, at[1]])
    arrive(T_SIB_M, text.at[o, at[1]])
    send(T_ON_M, text.at[o, at[1]], text.at[o, at[1]], down)
    chained(2, 2)

    def text_ready(part, r):
        t_high[part, at[r]], t_low[part, at[r]] = split(text[part, at[r]])

    def image_ready(k, part, r):
        cols = slice(k * piece, (k + 1) * piece)
        i_high[part, at[r], :, cols], i_low[part, at[r], :, cols] = split(image[k, part, at[r]])

    def image_sibling(k, r):
        arrive(I_SIB + 4 * k + r, image.at[k, o, at[r]])
        image_ready(k, o, r)

    text_ready(c, 0)
    text_ready(o, 0)
    text_ready(c, 3)
    text_ready(c, 1)
    text_ready(o, 1)
    for k in range(SHIFTS - 1):
        for r in (0, 3, 1, 2):
            image_ready(k, c, r)
            image_sibling(k, r)
    for r in (3, 1, 2):
        chained(3, r)
    for r in (0, 3, 1, 2):
        image_ready(3, c, r)
        image_sibling(3, r)
    arrive(T_SIB_P, text.at[o, at[3]])
    text_ready(o, 3)
    arrive(T_ON_P, text.at[c, at[2]])
    text_ready(c, 2)
    arrive(T_ON_M, text.at[o, at[2]])
    text_ready(o, 2)

    depth = 2 * N_Q * d
    th, tl = t_high[...].reshape(depth, half), t_low[...].reshape(depth, half)
    ih, il = i_high[...].reshape(depth, rows), i_low[...].reshape(depth, rows)
    dots = dot3(th, tl, ih, il, ((0,), (0,)))
    heat = jnp.exp(jnp.full((1, rows), heat_ref[0], F32))
    slope = jax.nn.sigmoid(heat * dots + bias_ref[0])
    text_id = lax.broadcasted_iota(jnp.int32, slope.shape, 0) + c * half
    image_id = lax.broadcasted_iota(jnp.int32, slope.shape, 1)
    match = (image_id < piece) & (text_id == image_id + q * piece)
    slope = heat * (slope - jnp.where(match, 1.0, 0.0).astype(F32))
    sh, sl = split(slope)

    def image_gradient(ks):
        lo, hi = ks[0] * piece, (ks[-1] + 1) * piece
        grad = dot3(th, tl, sh[:, lo:hi], sl[:, lo:hi], ((1,), (0,)))
        grad = grad.reshape(2, N_Q, d, hi - lo)
        for i, k in enumerate(ks):
            g_image[k] = grad[..., i * piece : (i + 1) * piece]
            send(G_SIB + k, g_image.at[k, o], g_other.at[k], sib)

    def text_gradient(r):
        for part in range(2):
            g_text[part, at[r]] = dot3(
                i_high[part, at[r]], i_low[part, at[r]], sh, sl, ((1,), (1,))
            )

    def add_sibling(k):
        arrive(G_SIB + k, g_other.at[k])
        g_image[k, c] += g_other[k]

    def returned(step, r):
        slot = back.at[step, at[r]]
        arrive(BACK + 4 * step + r, slot)
        slot[...] += g_image[2 - step, c, at[r]]

    order = (2, 1, 3, 0)
    image_gradient((2, 3))
    text_gradient(2)
    send(B_FAR_P, g_text.at[0, at[2]], far_in.at[0], up)
    send(B_FAR_M, g_text.at[1, at[2]], far_in.at[1], down)
    add_sibling(3)
    for r in order:
        send(BACK + r, g_image.at[3, c, at[r]], back.at[0, at[r]], after)
    text_gradient(1)
    send(B_NEAR_P, g_text.at[1, at[1]], near_in.at[0], up)
    text_gradient(3)
    send(B_NEAR_M, g_text.at[0, at[3]], near_in.at[1], down)
    image_gradient((0, 1))
    add_sibling(2)
    text_gradient(0)
    for r in order:
        returned(0, r)
        send(BACK + 4 + r, back.at[0, at[r]], back.at[1, at[r]], after)
    add_sibling(1)
    add_sibling(0)
    arrive(B_FAR_P, far_in.at[0])
    g_text[0, at[1]] += far_in[0]
    send(B_SUM_P, g_text.at[0, at[1]], near_in.at[2], up)
    arrive(B_FAR_M, far_in.at[1])
    g_text[1, at[3]] += far_in[1]
    send(B_SUM_M, g_text.at[1, at[3]], near_in.at[3], down)
    for r in order:
        returned(1, r)
        send(BACK + 8 + r, back.at[1, at[r]], back.at[2, at[r]], after)

    arrive(B_NEAR_P, near_in.at[0])
    arrive(B_NEAR_M, near_in.at[1])
    arrive(B_SUM_P, near_in.at[2])
    arrive(B_SUM_M, near_in.at[3])
    g_text[0, q] += near_in[1] + near_in[2]
    g_text[1, q] += near_in[0] + near_in[3]
    keep[...] = g_text[o, q]
    send(B_SIB, keep, half_of(gt_ref, c), sib)
    half_of(gt_ref, c)[...] = g_text[c, q]

    def own_columns(r, first=0, count=None):
        return piece_of(gi_ref, r, first, count)

    returned(2, 2)
    send(E_HALF_P, back.at[2, at[2], pl.ds(0, h)], half_in.at[2], up)
    send(E_HALF_M, back.at[2, at[2], pl.ds(h, h)], half_in.at[3], down)
    returned(2, 1)
    send(E_DIRECT_P, back.at[2, at[1]], own_columns(0), up)
    returned(2, 3)
    send(E_DIRECT_M, back.at[2, at[3]], own_columns(0), down)
    arrive(E_HALF_P, half_in.at[2])
    send(E_ON_P, half_in.at[2], own_columns(3, 0, h), up)
    arrive(E_HALF_M, half_in.at[3])
    send(E_ON_M, half_in.at[3], own_columns(1, h, h), down)
    returned(2, 0)
    own_columns(0)[...] = back[2, q]
    arrive(E_DIRECT_P, own_columns(3))
    arrive(E_DIRECT_M, own_columns(1))
    arrive(E_ON_P, own_columns(2, 0, h))
    arrive(E_ON_M, own_columns(2, h, h))
    arrive(B_SIB, half_of(gt_ref, o))
    for copy in started:
        copy.wait_send()


def shards(image_shard, text_shard, heat, bias):
    d, rows = image_shard.shape
    half, piece = rows // 2, rows // N_Q
    vmem = pl.BlockSpec(memory_space=pltpu.VMEM)
    smem = pl.BlockSpec(memory_space=pltpu.SMEM)
    n_dp = lax.axis_size("dp")

    def body(*refs):
        kernel(n_dp, *refs)

    return pl.pallas_call(
        body,
        out_shape=(jax.ShapeDtypeStruct((d, rows), F32), jax.ShapeDtypeStruct((d, rows), F32)),
        in_specs=[smem, smem, vmem, vmem],
        out_specs=(vmem, vmem),
        scratch_shapes=[
            pltpu.VMEM((2, N_Q, d, half), F32),
            pltpu.VMEM((SHIFTS, 2, N_Q, d, piece), F32),
            pltpu.VMEM((2, N_Q, d, half), BF16),
            pltpu.VMEM((2, N_Q, d, half), BF16),
            pltpu.VMEM((2, N_Q, d, rows), BF16),
            pltpu.VMEM((2, N_Q, d, rows), BF16),
            pltpu.VMEM((2, N_Q, d, half), F32),
            pltpu.VMEM((SHIFTS, 2, N_Q, d, piece), F32),
            pltpu.VMEM((SHIFTS, N_Q, d, piece), F32),
            pltpu.VMEM((SHIFTS - 1, N_Q, d, piece), F32),
            pltpu.VMEM((2, d, half), F32),
            pltpu.VMEM((4, d, half), F32),
            pltpu.VMEM((d, half), F32),
            pltpu.VMEM((4, d // 2, piece), F32),
            pltpu.SemaphoreType.DMA((N_SEMS,)),
            pltpu.SemaphoreType.DMA((N_SEMS,)),
        ],
        compiler_params=pltpu.CompilerParams(
            collective_id=0, has_side_effects=True, vmem_limit_bytes=48 * 2**20
        ),
        name="window_gradients",
    )(heat, bias, image_shard, text_shard)


def solution(mesh):
    return jax.shard_map(
        shards,
        mesh=mesh,
        in_specs=(P("tensor", "dp"), P("tensor", "dp"), P(), P()),
        out_specs=(P("tensor", "dp"), P("tensor", "dp")),
        check_vma=False,
    )
```

time: 252 us -> 97.5 us (0.39)
  the two profiles are of different devices: /device:TPU:128 before, /device:TPU:6 now
where the time goes in v1:
time: 97.5 us; the launch traced here: 97.3 us
  Pallas kernels  92.1 us (94%)
  local copies, waits for them, and re-layouts  3.35 us (3%)
  between operations  1.94 us (2%)
    pallas_call x1, Pallas kernels, shards(): pl.pallas_call(body, out_shape=(jax.ShapeDtypeStruct((d, rows), F32), jax...  92.1 us
    unnamed x6, local copies, waits for them, and re-layouts  3.35 us

profile of v1, /device:TPU:6, one launch (start us, length us, event | category | flops | bytes accessed | tf_op | source)
XLA Modules:
  0.0 97.3 jit_solution(6930898845082144171)
XLA Ops:
  1.9 0.0 copy-start
  1.9 1.0 copy-done
  2.9 0.0 copy-start.1
  2.9 1.0 copy-done.1
  3.8 92.1 %window_gradients.1 = (f32[144,512]{1,0:T(8,128)S(1)}, f32[144,512]{1,0:T(8,128)S(1)}) custom-call(f32[1]{0:T(128)S(6)} %copy.8.refs_0_, f32[1]{0:T(128)S(6)} %copy.9.refs_1_, f32[144,512]{1,0:T(8,128)S(1)} %copy-done, f32[144,512]{1,0:T(8,128)S(1)} %copy-done.1), custom_call_target="tpu_custom_call" | custom-call | tf_op jit(solution)/shard_map/window_gradients/pallas_call | solution.py:302
  95.9 0.7 copy.10
  96.6 0.7 copy.11
Async XLA Ops:
  1.9 1.0 copy-start
  2.9 1.0 copy-start.1

commit v2 on v1

--- a/solution.py
+++ b/solution.py
@@ -19,7 +19,14 @@
 I_SIB = 30
 CHAIN = 46
 BACK = 58
-N_SEMS = 70
+STOP = 70
+LAND = 82
+PAUSE = 86
+N_SEMS = 90
+
+HALF = 32
+BACK_STOP = 29
+STOPS = {3: 24, 1: 16, 2: 8, 4: 24, 7: 16, 5: 8, 10: 24, 8: 16, 11: 8}
 
 
 def split(value):
@@ -56,6 +63,9 @@
     near_in,
     keep,
     half_in,
+    stop,
+    landed,
+    pause,
     send_sem,
     recv_sem,
 ):
@@ -68,29 +78,31 @@
     sib = (dp, 2 * q + o)
     up, down = (dp, 2 * at[1] + c), (dp, 2 * at[3] + c)
     after, before = (lax.rem(dp + 1, n_dp), t), (lax.rem(dp + n_dp - 1, n_dp), t)
+    column = lax.rem(dp, HALF)
+    here = dp - column
+    there = HALF - here
     started = []
 
-    def send(index, src, dst, device):
-        copy = pltpu.make_async_remote_copy(
+    def remote(index, src, dst, device, landing=None):
+        return pltpu.make_async_remote_copy(
             src_ref=src,
             dst_ref=dst,
             send_sem=send_sem.at[index],
-            recv_sem=recv_sem.at[index],
+            recv_sem=recv_sem.at[index if landing is None else landing],
             device_id=device,
             device_id_type=MESH,
         )
+
+    def send(index, src, dst, device):
+        copy = remote(index, src, dst, device)
         copy.start()
         started.append(copy)
 
     def arrive(index, dst):
-        pltpu.make_async_remote_copy(
-            src_ref=dst,
-            dst_ref=dst,
-            send_sem=send_sem.at[index],
-            recv_sem=recv_sem.at[index],
-            device_id=sib,
-            device_id_type=MESH,
-        ).wait_recv()
+        remote(index, dst, dst, sib).wait_recv()
+
+    def member(block, r):
+        return (block, 2 * at[r] + c)
 
     def piece_of(ref, r, first=0, count=None):
         cols = pl.ds(pl.multiple_of(at[r] * piece, piece), piece)
@@ -103,21 +115,69 @@
     partners = (sib, up, down, after, before)
     for partner in partners:
         pl.semaphore_signal(barrier, inc=1, device_id=partner, device_id_type=MESH)
-    pl.semaphore_wait(barrier, len(partners))
+    greeted = len(partners)
+    edge = HALF - 1
+    meetings = [(k, there + edge, N_Q) for k in range(SHIFTS - 1)]
+    meetings += [(edge, there + k, N_Q) for k in range(SHIFTS - 1)]
+    for stop_at in sorted(set(STOPS.values())):
+        meetings += [(0, here + stop_at, 1), (stop_at, here, 1)]
+        meetings += [(edge, there + stop_at, 1), (stop_at, there + edge, 1)]
+    meetings += [(edge, here + BACK_STOP, 1), (BACK_STOP, here + edge, 1)]
+    meetings += [(BACK_STOP, there + SHIFTS - 2, N_Q), (SHIFTS - 2, there + BACK_STOP, N_Q)]
+    for where, block, count in meetings:
+
+        @pl.when(column == where)
+        def _():
+            for r in range(count):
+                pl.semaphore_signal(
+                    barrier, inc=1, device_id=member(block, r), device_id_type=MESH
+                )
+
+        greeted += jnp.where(column == where, count, 0)
+    pl.semaphore_wait(barrier, greeted)
 
     h = d // 2
     send(A_HALF_P, piece_of(img_ref, 2, 0, h), half_in.at[0], up)
     send(A_HALF_M, piece_of(img_ref, 2, h, h), half_in.at[1], down)
     image[0, c, q] = piece_of(img_ref, 0)[...]
 
+    inside = []
+
+    def opposite(r):
+        return (N_Q - r) % N_Q
+
     def chain(k, r):
         if k < SHIFTS - 1:
-            send(CHAIN + 4 * k + r, image.at[k, c, at[r]], image.at[k + 1, c, at[r]], before)
+            number = 4 * k + r
+            src, dst = image.at[k, c, at[r]], image.at[k + 1, c, at[r]]
+            copy = remote(CHAIN + number, src, dst, before)
+            started.append(copy)
+            if number in STOPS:
+                detour = remote(
+                    CHAIN + number, src, stop.at[number], (here + STOPS[number], t), STOP + number
+                )
+                pl.when(column != 0)(copy.start)
+                pl.when(column == 0)(detour.start)
+            else:
+                copy.start()
         send(I_SIB + 4 * k + r, image.at[k, c, at[r]], image.at[k, c, at[r]], sib)
 
     def chained(k, r):
         arrive(CHAIN + 4 * (k - 1) + r, image.at[k, c, at[r]])
         chain(k, r)
+
+    def pass_edge(k, r):
+        number = 4 * (k - 1) + r
+        if number in STOPS:
+            dst = image.at[k, c, at[r]]
+            copy = remote(STOP + number, stop.at[number], dst, (there + edge, t), CHAIN + number)
+
+            @pl.when(column == STOPS[number])
+            def _():
+                arrive(STOP + number, stop.at[number])
+                copy.start()
+
+            inside.append((column == STOPS[number], copy))
 
     chain(0, 0)
     send(A_DIRECT_P, piece_of(img_ref, 1), image.at[0, c, q], up)
@@ -132,6 +192,7 @@
     send(T_OWN_P, text.at[c, q], text.at[c, q], up)
     send(T_OWN_M, text.at[c, q], text.at[c, q], down)
 
+    pass_edge(1, 0)
     chained(1, 0)
     arrive(A_DIRECT_P, image.at[0, c, at[3]])
     chain(0, 3)
@@ -143,19 +204,29 @@
     arrive(A_ON_P, image.at[0, c, at[2], pl.ds(0, h)])
     arrive(A_ON_M, image.at[0, c, at[2], pl.ds(h, h)])
     chain(0, 2)
+    pass_edge(2, 0)
     chained(2, 0)
+    pass_edge(1, 3)
     chained(1, 3)
+    pass_edge(1, 1)
     chained(1, 1)
     arrive(T_OWN_P, text.at[c, at[3]])
     send(T_ON_P, text.at[c, at[3]], text.at[c, at[3]], up)
+    pass_edge(1, 2)
     chained(1, 2)
+    pass_edge(3, 0)
     chained(3, 0)
+    pass_edge(2, 3)
     chained(2, 3)
+    pass_edge(2, 1)
     chained(2, 1)
+    pass_edge(2, 2)
+    chained(2, 2)
     arrive(T_OWN_M, text.at[c, at[1]])
     arrive(T_SIB_M, text.at[o, at[1]])
     send(T_ON_M, text.at[o, at[1]], text.at[o, at[1]], down)
-    chained(2, 2)
+    for r in (3, 1, 2):
+        pass_edge(3, r)
 
     def text_ready(part, r):
         t_high[part, at[r]], t_low[part, at[r]] = split(text[part, at[r]])
@@ -219,10 +290,32 @@
         arrive(G_SIB + k, g_other.at[k])
         g_image[k, c] += g_other[k]
 
+    paused = []
+
+    def give_back(step, r, grad):
+        copy = remote(BACK + 4 * step + r, grad, back.at[step, at[r]], after)
+        pl.when(column != HALF - 1)(copy.start)
+        cols = pl.ds(pl.multiple_of(q * piece, piece), piece)
+        target = member(there + SHIFTS - 2 - step, r)
+        if step == 0:
+            leap = remote(BACK + r, grad, pause.at[r], (here + BACK_STOP, t), PAUSE + r)
+            onward = remote(PAUSE + r, pause.at[r], landed.at[:, cols], target, LAND + opposite(r))
+            paused.append(onward)
+        else:
+            leap = remote(
+                BACK + 4 * step + r, grad, landed.at[:, cols], target, LAND + opposite(r)
+            )
+        pl.when(column == HALF - 1)(leap.start)
+        started.append(copy)
+
     def returned(step, r):
         slot = back.at[step, at[r]]
-        arrive(BACK + 4 * step + r, slot)
+        pl.when(column != 0)(remote(BACK + 4 * step + r, slot, slot, sib).wait_recv)
         slot[...] += g_image[2 - step, c, at[r]]
+
+    @pl.when(column == 0)
+    def _():
+        back[...] = jnp.zeros_like(back)
 
     order = (2, 1, 3, 0)
     image_gradient((2, 3))
@@ -231,17 +324,25 @@
     send(B_FAR_M, g_text.at[1, at[2]], far_in.at[1], down)
     add_sibling(3)
     for r in order:
-        send(BACK + r, g_image.at[3, c, at[r]], back.at[0, at[r]], after)
+        give_back(0, r, g_image.at[3, c, at[r]])
     text_gradient(1)
     send(B_NEAR_P, g_text.at[1, at[1]], near_in.at[0], up)
     text_gradient(3)
     send(B_NEAR_M, g_text.at[0, at[3]], near_in.at[1], down)
     image_gradient((0, 1))
+
+    @pl.when(column == BACK_STOP)
+    def _():
+        for i, r in enumerate(order):
+            arrive(PAUSE + r, pause.at[r])
+            paused[i].start()
+
+    inside.extend((column == BACK_STOP, copy) for copy in paused)
     add_sibling(2)
     text_gradient(0)
     for r in order:
         returned(0, r)
-        send(BACK + 4 + r, back.at[0, at[r]], back.at[1, at[r]], after)
+        give_back(1, r, back.at[0, at[r]])
     add_sibling(1)
     add_sibling(0)
     arrive(B_FAR_P, far_in.at[0])
@@ -252,7 +353,7 @@
     send(B_SUM_M, g_text.at[1, at[3]], near_in.at[3], down)
     for r in order:
         returned(1, r)
-        send(BACK + 8 + r, back.at[1, at[r]], back.at[2, at[r]], after)
+        give_back(2, r, back.at[1, at[r]])
 
     arrive(B_NEAR_P, near_in.at[0])
     arrive(B_NEAR_M, near_in.at[1])
@@ -285,8 +386,17 @@
     arrive(E_ON_P, own_columns(2, 0, h))
     arrive(E_ON_M, own_columns(2, h, h))
     arrive(B_SIB, half_of(gt_ref, o))
+
+    @pl.when(column < SHIFTS - 1)
+    def _():
+        for r in range(N_Q):
+            arrive(LAND + r, piece_of(landed, r))
+        gi_ref[...] += landed[...]
+
     for copy in started:
         copy.wait_send()
+    for guard, copy in inside:
+        pl.when(guard)(copy.wait_send)
 
 
 def shards(image_shard, text_shard, heat, bias):
@@ -319,6 +429,9 @@
             pltpu.VMEM((4, d, half), F32),
             pltpu.VMEM((d, half), F32),
             pltpu.VMEM((4, d // 2, piece), F32),
+            pltpu.VMEM((4 * (SHIFTS - 1), d, piece), F32),
+            pltpu.VMEM((d, rows), F32),
+            pltpu.VMEM((N_Q, d, piece), F32),
             pltpu.SemaphoreType.DMA((N_SEMS,)),
             pltpu.SemaphoreType.DMA((N_SEMS,)),
         ],

time: 97.5 us -> 93.1 us (0.955)
  Pallas kernels: 92.1 us -> 87.6 us
    pallas_call x1, Pallas kernels: 92.1 us -> 87.6 us  [shards(): pl.pallas_call(body, out_shape=(jax.ShapeDtypeStruct((d, rows), F32), jax...]
where the time goes in v2:
time: 93.1 us; the launch traced here: 92.9 us
  Pallas kernels  87.6 us (94%)
  local copies, waits for them, and re-layouts  3.35 us (4%)
  between operations  1.94 us (2%)
    pallas_call x1, Pallas kernels, shards(): pl.pallas_call(body, out_shape=(jax.ShapeDtypeStruct((d, rows), F32), jax...  87.6 us
    unnamed x6, local copies, waits for them, and re-layouts  3.35 us

profile of v2, /device:TPU:6, one launch (start us, length us, event | category | flops | bytes accessed | tf_op | source)
XLA Modules:
  0.0 92.9 jit_solution(6453557728121469216)
XLA Ops:
  1.9 0.0 copy-start
  1.9 1.0 %copy-done = f32[144,512]{1,0:T(8,128)S(1)} copy-done((f32[144,512]{1,0:T(8,128)S(1)}, f32[144,512]{1,0:T(8,128)}, u32[]{:S(2)}) %copy-start) | copy-done | bytes 294936
  2.9 0.0 copy-start.1
  2.9 1.0 %copy-done.1 = f32[144,512]{1,0:T(8,128)S(1)} copy-done((f32[144,512]{1,0:T(8,128)S(1)}, f32[144,512]{1,0:T(8,128)}, u32[]{:S(2)}) %copy-start.1) | copy-done | bytes 294936
  3.8 87.6 %window_gradients.1 = (f32[144,512]{1,0:T(8,128)S(1)}, f32[144,512]{1,0:T(8,128)S(1)}) custom-call(f32[1]{0:T(128)S(6)} %copy.8.refs_0_, f32[1]{0:T(128)S(6)} %copy.9.refs_1_, f32[144,512]{1,0:T(8,128)S(1)} %copy-done, f32[144,512]{1,0:T(8,128)S(1)} %copy-done.1), custom_call_target="tpu_custom_call" | custom-call | tf_op jit(solution)/shard_map/window_gradients/pallas_call | solution.py:412
  91.5 0.7 copy.10
  92.2 0.7 copy.11
Async XLA Ops:
  1.9 1.0 %copy-start = (f32[144,512]{1,0:T(8,128)S(1)}, f32[144,512]{1,0:T(8,128)}, u32[]{:S(2)}) copy-start(f32[144,512]{1,0:T(8,128)} %refs_2_.1) | copy-start | bytes 884740
  2.9 1.0 %copy-start.1 = (f32[144,512]{1,0:T(8,128)S(1)}, f32[144,512]{1,0:T(8,128)}, u32[]{:S(2)}) copy-start(f32[144,512]{1,0:T(8,128)} %refs_3_.1) | copy-start | bytes 884740

commit v3 on v2

--- a/solution.py
+++ b/solution.py
@@ -22,11 +22,11 @@
 STOP = 70
 LAND = 82
 PAUSE = 86
-N_SEMS = 90
+N_SEMS = 98
 
 HALF = 32
-BACK_STOP = 29
-STOPS = {3: 24, 1: 16, 2: 8, 4: 24, 7: 16, 5: 8, 10: 24, 8: 16, 11: 8}
+BACK_STOPS = {1: 7, 3: 23, 0: 23, 5: 7, 7: 23, 4: 7, 9: 7, 8: 23}
+STOPS = {0: 24, 3: 16, 1: 8, 2: 24, 4: 16, 7: 8, 5: 24, 8: 16, 11: 8}
 
 
 def split(value):
@@ -63,11 +63,13 @@
     near_in,
     keep,
     half_in,
+    dots,
     stop,
     landed,
     pause,
     send_sem,
     recv_sem,
+    local_sem,
 ):
     d, rows = img_ref.shape
     half, piece = rows // 2, rows // N_Q
@@ -111,6 +113,10 @@
     def half_of(ref, which):
         return ref.at[:, pl.ds(pl.multiple_of(which * half, half), half)]
 
+    own_piece = pltpu.make_async_copy(piece_of(img_ref, 0), image.at[0, c, q], local_sem.at[0])
+    own_text = pltpu.make_async_copy(half_of(txt_ref, c), text.at[c, q], local_sem.at[1])
+    own_piece.start()
+    own_text.start()
     barrier = pltpu.get_barrier_semaphore()
     partners = (sib, up, down, after, before)
     for partner in partners:
@@ -122,8 +128,10 @@
     for stop_at in sorted(set(STOPS.values())):
         meetings += [(0, here + stop_at, 1), (stop_at, here, 1)]
         meetings += [(edge, there + stop_at, 1), (stop_at, there + edge, 1)]
-    meetings += [(edge, here + BACK_STOP, 1), (BACK_STOP, here + edge, 1)]
-    meetings += [(BACK_STOP, there + SHIFTS - 2, N_Q), (SHIFTS - 2, there + BACK_STOP, N_Q)]
+    for stop_at in sorted(set(BACK_STOPS.values())):
+        meetings += [(edge, here + stop_at, 1), (stop_at, here + edge, 1)]
+        for k in range(SHIFTS - 1):
+            meetings += [(stop_at, there + k, N_Q), (k, there + stop_at, N_Q)]
     for where, block, count in meetings:
 
         @pl.when(column == where)
@@ -139,7 +147,6 @@
     h = d // 2
     send(A_HALF_P, piece_of(img_ref, 2, 0, h), half_in.at[0], up)
     send(A_HALF_M, piece_of(img_ref, 2, h, h), half_in.at[1], down)
-    image[0, c, q] = piece_of(img_ref, 0)[...]
 
     inside = []
 
@@ -179,16 +186,17 @@
 
             inside.append((column == STOPS[number], copy))
 
+    own_piece.wait()
     chain(0, 0)
     send(A_DIRECT_P, piece_of(img_ref, 1), image.at[0, c, q], up)
     send(A_DIRECT_M, piece_of(img_ref, 3), image.at[0, c, q], down)
     send(T_SIB, half_of(txt_ref, o), text.at[c, q], sib)
-    text[c, q] = half_of(txt_ref, c)[...]
 
     arrive(A_HALF_P, half_in.at[0])
     send(A_ON_P, half_in.at[0], image.at[0, c, at[3], pl.ds(0, h)], up)
     arrive(A_HALF_M, half_in.at[1])
     send(A_ON_M, half_in.at[1], image.at[0, c, at[1], pl.ds(h, h)], down)
+    own_text.wait()
     send(T_OWN_P, text.at[c, q], text.at[c, q], up)
     send(T_OWN_M, text.at[c, q], text.at[c, q], down)
 
@@ -255,6 +263,16 @@
         image_sibling(3, r)
     arrive(T_SIB_P, text.at[o, at[3]])
     text_ready(o, 3)
+
+    def quarter_dots(r):
+        def rows_of(ref):
+            return ref[:, at[r]].reshape(2 * d, ref.shape[-1])
+
+        return dot3(
+            rows_of(t_high), rows_of(t_low), rows_of(i_high), rows_of(i_low), ((0,), (0,))
+        )
+
+    dots[...] = quarter_dots(0) + quarter_dots(3) + quarter_dots(1)
     arrive(T_ON_P, text.at[c, at[2]])
     text_ready(c, 2)
     arrive(T_ON_M, text.at[o, at[2]])
@@ -262,10 +280,8 @@
 
     depth = 2 * N_Q * d
     th, tl = t_high[...].reshape(depth, half), t_low[...].reshape(depth, half)
-    ih, il = i_high[...].reshape(depth, rows), i_low[...].reshape(depth, rows)
-    dots = dot3(th, tl, ih, il, ((0,), (0,)))
     heat = jnp.exp(jnp.full((1, rows), heat_ref[0], F32))
-    slope = jax.nn.sigmoid(heat * dots + bias_ref[0])
+    slope = jax.nn.sigmoid(heat * (dots[...] + quarter_dots(2)) + bias_ref[0])
     text_id = lax.broadcasted_iota(jnp.int32, slope.shape, 0) + c * half
     image_id = lax.broadcasted_iota(jnp.int32, slope.shape, 1)
     match = (image_id < piece) & (text_id == image_id + q * piece)
@@ -290,21 +306,35 @@
         arrive(G_SIB + k, g_other.at[k])
         g_image[k, c] += g_other[k]
 
-    paused = []
+    paused = {}
+
+    def give_on(step):
+        for r in order:
+            number = 4 * step + r
+            if number in BACK_STOPS:
+
+                @pl.when(column == BACK_STOPS[number])
+                def _():
+                    arrive(PAUSE + number, pause.at[number])
+                    paused[number].start()
 
     def give_back(step, r, grad):
         copy = remote(BACK + 4 * step + r, grad, back.at[step, at[r]], after)
         pl.when(column != HALF - 1)(copy.start)
         cols = pl.ds(pl.multiple_of(q * piece, piece), piece)
         target = member(there + SHIFTS - 2 - step, r)
-        if step == 0:
-            leap = remote(BACK + r, grad, pause.at[r], (here + BACK_STOP, t), PAUSE + r)
-            onward = remote(PAUSE + r, pause.at[r], landed.at[:, cols], target, LAND + opposite(r))
-            paused.append(onward)
+        number = 4 * step + r
+        if number in BACK_STOPS:
+            leap = remote(
+                BACK + number, grad, pause.at[number], (here + BACK_STOPS[number], t), PAUSE + number
+            )
+            onward = remote(
+                PAUSE + number, pause.at[number], landed.at[:, cols], target, LAND + opposite(r)
+            )
+            paused[number] = onward
+            inside.append((column == BACK_STOPS[number], onward))
         else:
-            leap = remote(
-                BACK + 4 * step + r, grad, landed.at[:, cols], target, LAND + opposite(r)
-            )
+            leap = remote(BACK + number, grad, landed.at[:, cols], target, LAND + opposite(r))
         pl.when(column == HALF - 1)(leap.start)
         started.append(copy)
 
@@ -318,7 +348,7 @@
         back[...] = jnp.zeros_like(back)
 
     order = (2, 1, 3, 0)
-    image_gradient((2, 3))
+    image_gradient((3,))
     text_gradient(2)
     send(B_FAR_P, g_text.at[0, at[2]], far_in.at[0], up)
     send(B_FAR_M, g_text.at[1, at[2]], far_in.at[1], down)
@@ -329,15 +359,8 @@
     send(B_NEAR_P, g_text.at[1, at[1]], near_in.at[0], up)
     text_gradient(3)
     send(B_NEAR_M, g_text.at[0, at[3]], near_in.at[1], down)
+    image_gradient((2,))
     image_gradient((0, 1))
-
-    @pl.when(column == BACK_STOP)
-    def _():
-        for i, r in enumerate(order):
-            arrive(PAUSE + r, pause.at[r])
-            paused[i].start()
-
-    inside.extend((column == BACK_STOP, copy) for copy in paused)
     add_sibling(2)
     text_gradient(0)
     for r in order:
@@ -354,6 +377,7 @@
     for r in order:
         returned(1, r)
         give_back(2, r, back.at[1, at[r]])
+    give_on(0)
 
     arrive(B_NEAR_P, near_in.at[0])
     arrive(B_NEAR_M, near_in.at[1])
@@ -364,6 +388,7 @@
     keep[...] = g_text[o, q]
     send(B_SIB, keep, half_of(gt_ref, c), sib)
     half_of(gt_ref, c)[...] = g_text[c, q]
+    give_on(1)
 
     def own_columns(r, first=0, count=None):
         return piece_of(gi_ref, r, first, count)
@@ -381,6 +406,7 @@
     send(E_ON_M, half_in.at[3], own_columns(1, h, h), down)
     returned(2, 0)
     own_columns(0)[...] = back[2, q]
+    give_on(2)
     arrive(E_DIRECT_P, own_columns(3))
     arrive(E_DIRECT_M, own_columns(1))
     arrive(E_ON_P, own_columns(2, 0, h))
@@ -404,6 +430,7 @@
     half, piece = rows // 2, rows // N_Q
     vmem = pl.BlockSpec(memory_space=pltpu.VMEM)
     smem = pl.BlockSpec(memory_space=pltpu.SMEM)
+    hbm = pl.BlockSpec(memory_space=pl.ANY)
     n_dp = lax.axis_size("dp")
 
     def body(*refs):
@@ -412,7 +439,7 @@
     return pl.pallas_call(
         body,
         out_shape=(jax.ShapeDtypeStruct((d, rows), F32), jax.ShapeDtypeStruct((d, rows), F32)),
-        in_specs=[smem, smem, vmem, vmem],
+        in_specs=[smem, smem, hbm, hbm],
         out_specs=(vmem, vmem),
         scratch_shapes=[
             pltpu.VMEM((2, N_Q, d, half), F32),
@@ -429,11 +456,13 @@
             pltpu.VMEM((4, d, half), F32),
             pltpu.VMEM((d, half), F32),
             pltpu.VMEM((4, d // 2, piece), F32),
+            pltpu.VMEM((half, rows), F32),
             pltpu.VMEM((4 * (SHIFTS - 1), d, piece), F32),
             pltpu.VMEM((d, rows), F32),
-            pltpu.VMEM((N_Q, d, piece), F32),
+            pltpu.VMEM((4 * (SHIFTS - 1), d, piece), F32),
             pltpu.SemaphoreType.DMA((N_SEMS,)),
             pltpu.SemaphoreType.DMA((N_SEMS,)),
+            pltpu.SemaphoreType.DMA((2,)),
         ],
         compiler_params=pltpu.CompilerParams(
             collective_id=0, has_side_effects=True, vmem_limit_bytes=48 * 2**20

time: 93.1 us -> 90 us (0.967)
  Pallas kernels: 87.6 us -> 84.5 us
    pallas_call x1, Pallas kernels: 87.6 us -> 84.5 us  [shards(): pl.pallas_call(body, out_shape=(jax.ShapeDtypeStruct((d, rows), F32), jax...]
where the time goes in v3:
time: 90 us; the launch traced here: 89.8 us
  Pallas kernels  84.5 us (94%)
  local copies, waits for them, and re-layouts  3.35 us (4%)
  between operations  1.94 us (2%)
    pallas_call x1, Pallas kernels, shards(): pl.pallas_call(body, out_shape=(jax.ShapeDtypeStruct((d, rows), F32), jax...  84.5 us
    unnamed x6, local copies, waits for them, and re-layouts  3.35 us

profile of v3, /device:TPU:6, one launch (start us, length us, event | category | flops | bytes accessed | tf_op | source)
XLA Modules:
  0.0 89.8 jit_solution(5571577119114497457)
XLA Ops:
  1.9 0.0 copy-start
  1.9 1.0 %copy-done = f32[144,512]{1,0:T(8,128)S(1)} copy-done((f32[144,512]{1,0:T(8,128)S(1)}, f32[144,512]{1,0:T(8,128)}, u32[]{:S(2)}) %copy-start) | copy-done | bytes 294936
  2.9 0.0 copy-start.1
  2.9 1.0 %copy-done.1 = f32[144,512]{1,0:T(8,128)S(1)} copy-done((f32[144,512]{1,0:T(8,128)S(1)}, f32[144,512]{1,0:T(8,128)}, u32[]{:S(2)}) %copy-start.1) | copy-done | bytes 294936
  3.8 84.5 %window_gradients.1 = (f32[144,512]{1,0:T(8,128)S(1)}, f32[144,512]{1,0:T(8,128)S(1)}) custom-call(f32[1]{0:T(128)S(6)} %copy.8.refs_0_, f32[1]{0:T(128)S(6)} %copy.9.refs_1_, f32[144,512]{1,0:T(8,128)S(1)} %copy-done, f32[144,512]{1,0:T(8,128)S(1)} %copy-done.1), custom_call_target="tpu_custom_call" | custom-call | tf_op jit(solution)/shard_map/window_gradients/pallas_call | solution.py:439
  88.4 0.7 copy.10
  89.1 0.7 copy.11
Async XLA Ops:
  1.9 1.0 %copy-start = (f32[144,512]{1,0:T(8,128)S(1)}, f32[144,512]{1,0:T(8,128)}, u32[]{:S(2)}) copy-start(f32[144,512]{1,0:T(8,128)} %refs_2_.1) | copy-start | bytes 884740
  2.9 1.0 %copy-start.1 = (f32[144,512]{1,0:T(8,128)S(1)}, f32[144,512]{1,0:T(8,128)}, u32[]{:S(2)}) copy-start(f32[144,512]{1,0:T(8,128)} %refs_3_.1) | copy-start | bytes 884740

commit v4 on v3

--- a/solution.py
+++ b/solution.py
@@ -297,10 +297,8 @@
             send(G_SIB + k, g_image.at[k, o], g_other.at[k], sib)
 
     def text_gradient(r):
-        for part in range(2):
-            g_text[part, at[r]] = dot3(
-                i_high[part, at[r]], i_low[part, at[r]], sh, sl, ((1,), (1,))
-            )
+        high, low = (ref[:, at[r]].reshape(2 * d, rows) for ref in (i_high, i_low))
+        g_text[:, at[r]] = dot3(high, low, sh_t, sl_t, ((1,), (0,))).reshape(2, d, half)
 
     def add_sibling(k):
         arrive(G_SIB + k, g_other.at[k])
@@ -349,6 +347,7 @@
 
     order = (2, 1, 3, 0)
     image_gradient((3,))
+    sh_t, sl_t = sh.T, sl.T
     text_gradient(2)
     send(B_FAR_P, g_text.at[0, at[2]], far_in.at[0], up)
     send(B_FAR_M, g_text.at[1, at[2]], far_in.at[1], down)

time: 90 us -> 89.3 us (level)
  no operation moved by 1% of the time
where the time goes in v4:
time: 89.3 us; the launch traced here: 89.1 us
  Pallas kernels  83.9 us (94%)
  local copies, waits for them, and re-layouts  3.35 us (4%)
  between operations  1.94 us (2%)
    pallas_call x1, Pallas kernels, shards(): pl.pallas_call(body, out_shape=(jax.ShapeDtypeStruct((d, rows), F32), jax...  83.9 us
    unnamed x6, local copies, waits for them, and re-layouts  3.35 us

profile of v4, /device:TPU:6, one launch (start us, length us, event | category | flops | bytes accessed | tf_op | source)
XLA Modules:
  0.0 89.1 jit_solution(4154797125552132997)
XLA Ops:
  1.9 0.0 copy-start
  1.9 1.0 %copy-done = f32[144,512]{1,0:T(8,128)S(1)} copy-done((f32[144,512]{1,0:T(8,128)S(1)}, f32[144,512]{1,0:T(8,128)}, u32[]{:S(2)}) %copy-start) | copy-done | bytes 294936
  2.9 0.0 copy-start.1
  2.9 1.0 %copy-done.1 = f32[144,512]{1,0:T(8,128)S(1)} copy-done((f32[144,512]{1,0:T(8,128)S(1)}, f32[144,512]{1,0:T(8,128)}, u32[]{:S(2)}) %copy-start.1) | copy-done | bytes 294936
  3.8 83.9 %window_gradients.1 = (f32[144,512]{1,0:T(8,128)S(1)}, f32[144,512]{1,0:T(8,128)S(1)}) custom-call(f32[1]{0:T(128)S(6)} %copy.8.refs_0_, f32[1]{0:T(128)S(6)} %copy.9.refs_1_, f32[144,512]{1,0:T(8,128)S(1)} %copy-done, f32[144,512]{1,0:T(8,128)S(1)} %copy-done.1), custom_call_target="tpu_custom_call" | custom-call | tf_op jit(solution)/shard_map/window_gradients/pallas_call | solution.py:438
  87.7 0.7 copy.10
  88.4 0.7 copy.11
Async XLA Ops:
  1.9 1.0 %copy-start = (f32[144,512]{1,0:T(8,128)S(1)}, f32[144,512]{1,0:T(8,128)}, u32[]{:S(2)}) copy-start(f32[144,512]{1,0:T(8,128)} %refs_2_.1) | copy-start | bytes 884740
  2.9 1.0 %copy-start.1 = (f32[144,512]{1,0:T(8,128)S(1)}, f32[144,512]{1,0:T(8,128)}, u32[]{:S(2)}) copy-start(f32[144,512]{1,0:T(8,128)} %refs_3_.1) | copy-start | bytes 884740

commit v5 on v4

--- a/solution.py
+++ b/solution.py
@@ -22,11 +22,12 @@
 STOP = 70
 LAND = 82
 PAUSE = 86
-N_SEMS = 98
+G_PART = 98
+N_SEMS = 102
 
 HALF = 32
 BACK_STOPS = {1: 7, 3: 23, 0: 23, 5: 7, 7: 23, 4: 7, 9: 7, 8: 23}
-STOPS = {0: 24, 3: 16, 1: 8, 2: 24, 4: 16, 7: 8, 5: 24, 8: 16, 11: 8}
+STOPS = {0: 24, 3: 16, 1: 8, 2: 24, 4: 24, 7: 8, 8: 16, 11: 8}
 
 
 def split(value):
@@ -198,7 +199,8 @@
     send(A_ON_M, half_in.at[1], image.at[0, c, at[1], pl.ds(h, h)], down)
     own_text.wait()
     send(T_OWN_P, text.at[c, q], text.at[c, q], up)
-    send(T_OWN_M, text.at[c, q], text.at[c, q], down)
+    arrive(T_SIB, text.at[o, q])
+    send(T_SIB_M, text.at[o, q], text.at[o, q], down)
 
     pass_edge(1, 0)
     chained(1, 0)
@@ -206,9 +208,8 @@
     chain(0, 3)
     arrive(A_DIRECT_M, image.at[0, c, at[1]])
     chain(0, 1)
-    arrive(T_SIB, text.at[o, q])
     send(T_SIB_P, text.at[o, q], text.at[o, q], up)
-    send(T_SIB_M, text.at[o, q], text.at[o, q], down)
+    send(T_OWN_M, text.at[c, q], text.at[c, q], down)
     arrive(A_ON_P, image.at[0, c, at[2], pl.ds(0, h)])
     arrive(A_ON_M, image.at[0, c, at[2], pl.ds(h, h)])
     chain(0, 2)
@@ -220,6 +221,8 @@
     chained(1, 1)
     arrive(T_OWN_P, text.at[c, at[3]])
     send(T_ON_P, text.at[c, at[3]], text.at[c, at[3]], up)
+    arrive(T_SIB_M, text.at[o, at[1]])
+    send(T_ON_M, text.at[o, at[1]], text.at[o, at[1]], down)
     pass_edge(1, 2)
     chained(1, 2)
     pass_edge(3, 0)
@@ -230,9 +233,6 @@
     chained(2, 1)
     pass_edge(2, 2)
     chained(2, 2)
-    arrive(T_OWN_M, text.at[c, at[1]])
-    arrive(T_SIB_M, text.at[o, at[1]])
-    send(T_ON_M, text.at[o, at[1]], text.at[o, at[1]], down)
     for r in (3, 1, 2):
         pass_edge(3, r)
 
@@ -250,7 +250,6 @@
     text_ready(c, 0)
     text_ready(o, 0)
     text_ready(c, 3)
-    text_ready(c, 1)
     text_ready(o, 1)
     for k in range(SHIFTS - 1):
         for r in (0, 3, 1, 2):
@@ -263,6 +262,8 @@
         image_sibling(3, r)
     arrive(T_SIB_P, text.at[o, at[3]])
     text_ready(o, 3)
+    arrive(T_OWN_M, text.at[c, at[1]])
+    text_ready(c, 1)
 
     def quarter_dots(r):
         def rows_of(ref):
@@ -288,13 +289,19 @@
     slope = heat * (slope - jnp.where(match, 1.0, 0.0).astype(F32))
     sh, sl = split(slope)
 
+    order = (2, 1, 3, 0)
+
     def image_gradient(ks):
         lo, hi = ks[0] * piece, (ks[-1] + 1) * piece
         grad = dot3(th, tl, sh[:, lo:hi], sl[:, lo:hi], ((1,), (0,)))
         grad = grad.reshape(2, N_Q, d, hi - lo)
         for i, k in enumerate(ks):
             g_image[k] = grad[..., i * piece : (i + 1) * piece]
-            send(G_SIB + k, g_image.at[k, o], g_other.at[k], sib)
+            if k < 3:
+                send(G_SIB + k, g_image.at[k, o], g_other.at[k], sib)
+                continue
+            for r in order:
+                send(G_PART + r, g_image.at[k, o, at[r]], g_other.at[k, at[r]], sib)
 
     def text_gradient(r):
         high, low = (ref[:, at[r]].reshape(2 * d, rows) for ref in (i_high, i_low))
@@ -345,14 +352,14 @@
     def _():
         back[...] = jnp.zeros_like(back)
 
-    order = (2, 1, 3, 0)
-    image_gradient((3,))
     sh_t, sl_t = sh.T, sl.T
     text_gradient(2)
     send(B_FAR_P, g_text.at[0, at[2]], far_in.at[0], up)
     send(B_FAR_M, g_text.at[1, at[2]], far_in.at[1], down)
-    add_sibling(3)
+    image_gradient((3,))
     for r in order:
+        arrive(G_PART + r, g_other.at[3, at[r]])
+        g_image[3, c, at[r]] += g_other[3, at[r]]
         give_back(0, r, g_image.at[3, c, at[r]])
     text_gradient(1)
     send(B_NEAR_P, g_text.at[1, at[1]], near_in.at[0], up)

time: 89.3 us -> 88.4 us (0.990)
  Pallas kernels: 83.9 us -> 82.4 us
    pallas_call x1, Pallas kernels: 83.9 us -> 82.4 us  [shards(): pl.pallas_call(body, out_shape=(jax.ShapeDtypeStruct((d, rows), F32), jax...]
where the time goes in v5:
time: 88.4 us; the launch traced here: 87.7 us
  Pallas kernels  82.4 us (93%)
  local copies, waits for them, and re-layouts  3.35 us (4%)
  between operations  1.94 us (2%)
    pallas_call x1, Pallas kernels, shards(): pl.pallas_call(body, out_shape=(jax.ShapeDtypeStruct((d, rows), F32), jax...  82.4 us
    unnamed x6, local copies, waits for them, and re-layouts  3.35 us

profile of v5, /device:TPU:6, one launch (start us, length us, event | category | flops | bytes accessed | tf_op | source)
XLA Modules:
  0.0 87.7 jit_solution(8805528938776829765)
XLA Ops:
  1.9 0.0 copy-start
  1.9 1.0 %copy-done = f32[144,512]{1,0:T(8,128)S(1)} copy-done((f32[144,512]{1,0:T(8,128)S(1)}, f32[144,512]{1,0:T(8,128)}, u32[]{:S(2)}) %copy-start) | copy-done | bytes 294936
  2.9 0.0 copy-start.1
  2.9 1.0 %copy-done.1 = f32[144,512]{1,0:T(8,128)S(1)} copy-done((f32[144,512]{1,0:T(8,128)S(1)}, f32[144,512]{1,0:T(8,128)}, u32[]{:S(2)}) %copy-start.1) | copy-done | bytes 294936
  3.8 82.4 %window_gradients.1 = (f32[144,512]{1,0:T(8,128)S(1)}, f32[144,512]{1,0:T(8,128)S(1)}) custom-call(f32[1]{0:T(128)S(6)} %copy.8.refs_0_, f32[1]{0:T(128)S(6)} %copy.9.refs_1_, f32[144,512]{1,0:T(8,128)S(1)} %copy-done, f32[144,512]{1,0:T(8,128)S(1)} %copy-done.1), custom_call_target="tpu_custom_call" | custom-call | tf_op jit(solution)/shard_map/window_gradients/pallas_call | solution.py:445
  86.3 0.7 copy.10
  87.0 0.7 copy.11
Async XLA Ops:
  1.9 1.0 %copy-start = (f32[144,512]{1,0:T(8,128)S(1)}, f32[144,512]{1,0:T(8,128)}, u32[]{:S(2)}) copy-start(f32[144,512]{1,0:T(8,128)} %refs_2_.1) | copy-start | bytes 884740
  2.9 1.0 %copy-start.1 = (f32[144,512]{1,0:T(8,128)S(1)}, f32[144,512]{1,0:T(8,128)}, u32[]{:S(2)}) copy-start(f32[144,512]{1,0:T(8,128)} %refs_3_.1) | copy-start | bytes 884740

commit v6 on v5

--- a/solution.py
+++ b/solution.py
@@ -27,7 +27,7 @@
 
 HALF = 32
 BACK_STOPS = {1: 7, 3: 23, 0: 23, 5: 7, 7: 23, 4: 7, 9: 7, 8: 23}
-STOPS = {0: 24, 3: 16, 1: 8, 2: 24, 4: 24, 7: 8, 8: 16, 11: 8}
+STOPS = {0: 24, 3: 16, 1: 8, 2: 24, 4: 24, 7: 8, 8: 24, 11: 8}
 
 
 def split(value):

time: 88.4 us -> 90 us (1.018)
  Pallas kernels: 82.4 us -> 84.5 us
    pallas_call x1, Pallas kernels: 82.4 us -> 84.5 us  [shards(): pl.pallas_call(body, out_shape=(jax.ShapeDtypeStruct((d, rows), F32), jax...]
where the time goes in v6:
time: 90 us; the launch traced here: 89.8 us
  Pallas kernels  84.5 us (94%)
  local copies, waits for them, and re-layouts  3.35 us (4%)
  between operations  1.94 us (2%)
    pallas_call x1, Pallas kernels, shards(): pl.pallas_call(body, out_shape=(jax.ShapeDtypeStruct((d, rows), F32), jax...  84.5 us
    unnamed x6, local copies, waits for them, and re-layouts  3.35 us

profile of v6, /device:TPU:6, one launch (start us, length us, event | category | flops | bytes accessed | tf_op | source)
XLA Modules:
  0.0 89.8 jit_solution(11677026626158200038)
XLA Ops:
  1.9 0.0 copy-start
  1.9 1.0 %copy-done = f32[144,512]{1,0:T(8,128)S(1)} copy-done((f32[144,512]{1,0:T(8,128)S(1)}, f32[144,512]{1,0:T(8,128)}, u32[]{:S(2)}) %copy-start) | copy-done | bytes 294936
  2.9 0.0 copy-start.1
  2.9 1.0 %copy-done.1 = f32[144,512]{1,0:T(8,128)S(1)} copy-done((f32[144,512]{1,0:T(8,128)S(1)}, f32[144,512]{1,0:T(8,128)}, u32[]{:S(2)}) %copy-start.1) | copy-done | bytes 294936
  3.8 84.5 %window_gradients.1 = (f32[144,512]{1,0:T(8,128)S(1)}, f32[144,512]{1,0:T(8,128)S(1)}) custom-call(f32[1]{0:T(128)S(6)} %copy.8.refs_0_, f32[1]{0:T(128)S(6)} %copy.9.refs_1_, f32[144,512]{1,0:T(8,128)S(1)} %copy-done, f32[144,512]{1,0:T(8,128)S(1)} %copy-done.1), custom_call_target="tpu_custom_call" | custom-call | tf_op jit(solution)/shard_map/window_gradients/pallas_call | solution.py:445
  88.3 0.7 copy.10
  89.1 0.7 copy.11
Async XLA Ops:
  1.9 1.0 %copy-start = (f32[144,512]{1,0:T(8,128)S(1)}, f32[144,512]{1,0:T(8,128)}, u32[]{:S(2)}) copy-start(f32[144,512]{1,0:T(8,128)} %refs_2_.1) | copy-start | bytes 884740
  2.9 1.0 %copy-start.1 = (f32[144,512]{1,0:T(8,128)S(1)}, f32[144,512]{1,0:T(8,128)}, u32[]{:S(2)}) copy-start(f32[144,512]{1,0:T(8,128)} %refs_3_.1) | copy-start | bytes 884740
